TPU v7x, 256 devices: a whole 4x4x8 slice. The times are simulated.
256 devices in a mesh: group: 8 (over z), dev: 32 (over x, y, core).
Axes of the slice: x: 4, y: 4, z: 8, core: 2. Of those that a mesh axis runs over, the one named last changes fastest.
Arguments:
- corpus_rows: bfloat16 [524288, 1024], P(('group', 'dev')), may hold values from -16 to 16
- list_ids: int32 [524288], P(('group', 'dev')), may hold values from 0 to 65535, as said below
- source_ids: int32 [524288], P(('group', 'dev')), may hold values from 0 to 999999
- list_slot: int32 [65536], replicated, may hold values from 0 to 65535, as said below
- centroids: bfloat16 [65536, 1024], P('dev'), may hold values from -13 to 13
- start_basis: float32 [1024, 256], replicated, may hold values from -6 to 6
Outputs:
- row_codes: bfloat16 [1310720, 256], P(('group', 'dev'))
- row_sources: int32 [1310720], P(('group', 'dev'))
- list_counts: int32 [65536], P('dev')
Inputs may be any that keep to these rules, and one draw needn't show every extreme that they name: A permutation; the centroid of list l is row list_slot[l] of centroids. For each device, at most 160 of its rows have an owner list_slot[list_ids] // 2048 equal to any one index o; in every draw one owner of each group takes exactly 160 rows from every device of that group.
All inputs are finite; a program needn't handle non-finite values.
Results may differ from a plain program's by a relative error of at most 0.001.
Values may be sent and summed in bfloat16 or wider, within the bound.
A program may use at most 128 MiB of HBM per device.

v0:
```python
import jax
import jax.numpy as jnp
from jax import lax
from jax.sharding import PartitionSpec as P

ITERS = 2


exact_mode = lax.Precision.HIGHEST


def orthonormal(product):
    gram_matrix = jnp.dot(
        product.T, product, precision=exact_mode, preferred_element_type=jnp.float32
    )
    factor = jnp.linalg.cholesky(gram_matrix)
    return jax.scipy.linalg.solve_triangular(factor, product.T, lower=True).T


def shards(corpus_rows, list_ids, source_ids, list_slot, centroids, start_basis):
    owner_total = lax.axis_size("dev")
    row_count, feature_dim = corpus_rows.shape
    lists_dev = centroids.shape[0]
    code_width = start_basis.shape[1]
    capacity = 5 * row_count // (2 * owner_total)
    basis_now = start_basis
    partial_value = lax.dot_general(
        corpus_rows, corpus_rows, (((0,), (0,)), ((), ())), preferred_element_type=jnp.float32
    )
    moment = lax.psum(partial_value, ("group", "dev"))
    for sweep in range(ITERS):
        product = jnp.dot(
            moment, basis_now, precision=exact_mode, preferred_element_type=jnp.float32
        )
        basis_now = orthonormal(product)
    slot_ids = jnp.take(list_slot, list_ids)
    owner_of = slot_ids // lists_dev
    local_ids = slot_ids % lists_dev
    owner_hits = (owner_of[:, None] == jnp.arange(owner_total, dtype=jnp.int32)[None, :]).astype(
        jnp.int32
    )
    order_rank = jnp.sum(owner_hits * (jnp.cumsum(owner_hits, axis=0) - 1), axis=1)
    position = owner_of * capacity + order_rank
    local_buffer = (
        jnp.full((owner_total * capacity,), -1, jnp.int32)
        .at[position]
        .set(local_ids)
        .reshape(owner_total, capacity)
    )
    source_buffer = (
        jnp.full((owner_total * capacity,), -1, jnp.int32)
        .at[position]
        .set(source_ids)
        .reshape(owner_total, capacity)
    )
    projected = jnp.dot(
        corpus_rows, basis_now, precision=exact_mode, preferred_element_type=jnp.float32
    )
    coded_buffer = (
        jnp.zeros((owner_total * capacity, code_width), jnp.float32)
        .at[position]
        .set(projected)
        .reshape(owner_total, capacity, code_width)
    )
    offsets = jnp.dot(
        centroids, basis_now, precision=exact_mode, preferred_element_type=jnp.float32
    )
    values = lax.all_to_all(coded_buffer, "dev", split_axis=0, concat_axis=0, tiled=True)
    arrived_ids = lax.all_to_all(local_buffer, "dev", split_axis=0, concat_axis=0, tiled=True)
    arrived_sources = lax.all_to_all(source_buffer, "dev", split_axis=0, concat_axis=0, tiled=True)
    filled = arrived_ids >= 0
    clamped = jnp.maximum(arrived_ids, 0)
    encoded = values - jnp.take(offsets, clamped, axis=0)
    codes_in = jnp.where(filled[..., None], encoded, 0.0).astype(jnp.bfloat16)
    filled_flat = (arrived_ids >= 0).astype(jnp.float32).reshape(-1)
    tallies = jax.ops.segment_sum(
        filled_flat, jnp.maximum(arrived_ids, 0).reshape(-1), num_segments=lists_dev
    )
    list_counts = lax.psum(tallies, "group").astype(jnp.int32)
    row_codes = codes_in.reshape(owner_total * capacity, code_width)
    row_sources = arrived_sources.reshape(owner_total * capacity)
    return (row_codes, row_sources, list_counts)


def solution(mesh):
    placed = (
        P(("group", "dev"), None),
        P(("group", "dev")),
        P(("group", "dev")),
        P(),
        P("dev", None),
        P(),
    )
    return jax.shard_map(
        shards,
        mesh=mesh,
        in_specs=placed,
        out_specs=(P(("group", "dev"), None), P(("group", "dev")), P("dev")),
        check_vma=False,
    )
```

profile of v0, /device:TPU:8, one launch (start us, length us, event | category | flops | bytes accessed | tf_op | source)
XLA Modules:
  0.0 572.3 jit_solution(12327310928597553631)
XLA Ops:
  7.2 10.1 %fusion.44 = f32[1024,1024]{1,0:T(8,128)} fusion(bf16[2048,1024]{1,0:T(8,128)(2,1)} %param.9), kind=kOutput, calls=%fused_computation.103 | convolution fusion | flops 4294967296 | bytes 8388608 | tf_op jit(solution)/shard_map/dot_general | solution.py:27
  17.3 0.7 copy-done.2
  18.3 11.8 %gather_fusion = s32[2048]{0:T(1024)S(1)} fusion(s32[65536]{0:T(1024)S(1)} %copy-done.1, s32[2048]{0:T(1024)S(1)} %fusion.34), kind=kCustom, calls=%fused_computation | custom fusion | bytes 24576 | tf_op jit(solution)/shard_map/jit(_take)/gather | solution.py:36
  30.1 9.1 %reduce-window.6 = s32[32,16,128]{2,1,0:T(8,128)S(1)} reduce-window(s32[32,16,128]{2,1,0:T(8,128)S(1)} %fusion.14, s32[]{:T(128)} %constant.122.clone.1), window={size=1x1x128 pad=0_0x0_0x127_0}, to_apply=%region_0.0 | reduce-window | flops 8323072 | bytes 524292 | tf_op jit(solution)/shard_map/reduce-window
  40.0 8.1 %scatter_custom_fusion = s32[5120]{0:T(1024)S(1)} fusion(s32[2048]{0:T(1024)S(1)} %compare_select_fusion, s32[2048]{0:T(1024)S(1)} %get-tuple-element.52, s32[]{:T(128)} %constant.121.clone.1), kind=kCustom, calls=%fused_computation.79 | custom fusion | bytes 20484 | tf_op jit(solution)/shard_map/scatter | solution.py:47
  48.1 0.7 all_to_all.15
  48.8 7.5 %all-to-all-start = ((s32[32,1,160]{2,1,0:T(1,128)}), s32[32,1,160]{2,1,0:T(1,128)S(1)}, u32[]{:S(2)}, u32[]{:S(2)}) async-start(s32[32,1,160]{2,1,0:T(1,128)} %all_to_all.15), calls=%async_computation | async-start | bytes 65536 | tf_op jit(solution)/shard_map/all_to_all | solution.py:69
  56.4 8.2 %scatter_custom_fusion.2 = s32[5120]{0:T(1024)S(1)} fusion(s32[2048]{0:T(1024)S(1)} %compare_select_fusion, s32[2048]{0:T(1024)} %param.11, s32[]{:T(128)} %constant.121.clone.1), kind=kCustom, calls=%fused_computation.77 | custom fusion | bytes 20992 | tf_op jit(solution)/shard_map/scatter | solution.py:53
  64.6 0.7 all_to_all.18
  65.3 223.7 %all-reduce.3.cloned.1.call-done = f32[1024,1024]{1,0:T(8,128)} async-done(((f32[1024,1024]{1,0:T(8,128)}), f32[1024,1024]{1,0:T(8,128)}) %all-reduce.3.cloned.1.call-update) | async-done | bytes 4194320 | tf_op jit(solution)/shard_map/psum | solution.py:30
  289.0 5.6 fusion.45
  294.6 1.8 fusion.46
  296.7 11.7 %cholesky.130 = f32[128,128]{1,0:T(8,128)S(1)} custom-call(f32[128,128]{1,0:T(8,128)S(1)} %cholesky.194), custom_call_target="Cholesky" | custom-call | tf_op jit(solution)/shard_map/jit(cholesky)/cholesky | solution.py:16
  308.4 9.8 %custom-call.13 = f32[1,128,128]{1,2,0:T(8,128)S(1)} custom-call(f32[1,128,128]{2,1,0:T(8,128)S(1)} %get-tuple-element.50), custom_call_target="InvertDiagBlocksLowerTriangular" | custom-call | tf_op jit(solution)/shard_map/jit(cholesky)/cholesky | solution.py:16
  318.7 11.7 %cholesky.147 = f32[128,128]{1,0:T(8,128)S(1)} custom-call(f32[128,128]{1,0:T(8,128)S(1)} %convolution_subtract_fusion.3), custom_call_target="Cholesky" | custom-call | tf_op jit(solution)/shard_map/jit(cholesky)/cholesky | solution.py:16
  330.5 0.7 compare_reduce_fusion.2
  345.5 3.9 while.4
  346.1 1.4 bitcast_dynamic-update-slice_fusion.4
  348.0 1.4 bitcast_dynamic-update-slice_fusion.4
  349.4 19.7 %custom-call.14 = f32[2,128,128]{1,2,0:T(8,128)S(1)} custom-call(f32[2,128,128]{2,1,0:T(8,128)S(1)} %get-tuple-element.19), custom_call_target="InvertDiagBlocksLowerTriangular" | custom-call | tf_op jit(solution)/shard_map/jit(_solve_triangular)/triangular_solve | solution.py:17
  369.1 0.6 fusion.8
  369.7 1.0 convolution_subtract_fusion.1
  370.7 0.6 fusion.20
  371.4 5.3 fusion.2
  376.7 1.8 fusion.47
  378.8 11.7 %cholesky.164 = f32[128,128]{1,0:T(8,128)S(1)} custom-call(f32[128,128]{1,0:T(8,128)S(1)} %cholesky.197), custom_call_target="Cholesky" | custom-call | tf_op jit(solution)/shard_map/jit(cholesky)/cholesky | solution.py:16
  390.5 9.8 %custom-call.15 = f32[1,128,128]{1,2,0:T(8,128)S(1)} custom-call(f32[1,128,128]{2,1,0:T(8,128)S(1)} %get-tuple-element.46), custom_call_target="InvertDiagBlocksLowerTriangular" | custom-call | tf_op jit(solution)/shard_map/jit(cholesky)/cholesky | solution.py:16
  400.8 11.7 %cholesky.181 = f32[128,128]{1,0:T(8,128)S(1)} custom-call(f32[128,128]{1,0:T(8,128)S(1)} %convolution_subtract_fusion.2), custom_call_target="Cholesky" | custom-call | tf_op jit(solution)/shard_map/jit(cholesky)/cholesky | solution.py:16
  412.5 0.6 compare_reduce_fusion.1
  413.2 0.6 compare_reduce_fusion
  415.6 4.0 while.5
  416.2 1.4 bitcast_dynamic-update-slice_fusion.5
  418.2 1.4 bitcast_dynamic-update-slice_fusion.5
  419.6 19.7 %custom-call.16 = f32[2,128,128]{1,2,0:T(8,128)S(1)} custom-call(f32[2,128,128]{2,1,0:T(8,128)S(1)} %get-tuple-element.20), custom_call_target="InvertDiagBlocksLowerTriangular" | custom-call | tf_op jit(solution)/shard_map/jit(_solve_triangular)/triangular_solve | solution.py:17
  440.0 1.0 convolution_subtract_fusion
  441.0 0.6 fusion.16
  441.6 7.0 %all-to-all-start.2 = ((s32[32,1,160]{2,1,0:T(1,128)}), s32[32,1,160]{2,1,0:T(1,128)S(1)}, u32[]{:S(2)}, u32[]{:S(2)}) async-start(s32[32,1,160]{2,1,0:T(1,128)} %all_to_all.18), calls=%async_computation.2 | async-start | bytes 65536 | tf_op jit(solution)/shard_map/all_to_all | solution.py:70
  448.6 7.0 %convolution_bitcast_fusion.1 = f32[2048,256]{0,1:T(8,128)} fusion(bf16[2048,1024]{1,0:T(8,128)(2,1)} %param.9, f32[128,1024]{1,0:T(8,128)S(1)} %fusion.16, f32[128,1024]{1,0:T(8,128)S(1)} %fusion.6), kind=kOutput, calls=%fused_computation.12 | convolution fusion | flops 6442713088 | bytes 7340032 | tf_op jit(solution)/shard_map/dot_general | solution.py:56
  455.5 2.9 copy.34
  458.5 12.1 %scatter_custom_fusion.1 = f32[5120,256]{1,0:T(8,128)} fusion(s32[2048]{0:T(1024)S(1)} %compare_select_fusion, f32[2048,256]{1,0:T(8,128)} %copy.34, f32[]{:T(128)} %constant.132.clone.1), kind=kCustom, calls=%fused_computation.13 | custom fusion | bytes 5243392 | tf_op jit(solution)/shard_map/scatter | solution.py:62
  470.5 7.4 %all-to-all-start.1 = ((f32[32,160,256]{2,1,0:T(8,128)}), f32[32,160,256]{2,1,0:T(8,128)}, u32[]{:S(2)}, u32[]{:S(2)}) async-start(f32[32,160,256]{2,1,0:T(8,128)} %bitcast.107), calls=%async_computation.1 | async-start | bytes 10485760 | tf_op jit(solution)/shard_map/all_to_all | solution.py:68
  478.1 0.7 reshape.138
  478.9 33.2 %scatter_custom_fusion.3 = f32[2048]{0:T(1024)S(1)} fusion(s32[5120]{0:T(1024)S(1)} %reshape.172, f32[5120]{0:T(1024)S(1)} %reshape.206, f32[]{:T(128)} %constant.132.clone.1), kind=kCustom, calls=%fused_computation.86 | custom fusion | flops 5120 | bytes 8196 | tf_op jit(solution)/shard_map/scatter-add | solution.py:76
  512.1 16.2 %psum.15 = f32[2048]{0:T(1024)S(1)} all-reduce(f32[2048]{0:T(1024)S(1)} %scatter_custom_fusion.3), channel_id=1, replica_groups=mesh['group'=8,'dev'=32] {'group'}, use_global_device_ids=true, to_apply=%region_12.15 | all-reduce | flops 2048 | bytes 16384 | tf_op jit(solution)/shard_map/psum | solution.py:79
  529.0 6.9 %convolution_bitcast_fusion = f32[2048,256]{0,1:T(8,128)} fusion(bf16[2048,1024]{1,0:T(8,128)(2,1)} %param.13, f32[128,1024]{1,0:T(8,128)S(1)} %fusion.16, f32[128,1024]{1,0:T(8,128)S(1)} %fusion.6), kind=kOutput, calls=%fused_computation.11 | convolution fusion | flops 6442713088 | bytes 7340032 | tf_op jit(solution)/shard_map/dot_general | solution.py:65
  535.9 1.9 copy.36
  537.8 20.0 %gather_fusion.1 = f32[5120,256]{1,0:T(8,128)} fusion(f32[2048,256]{1,0:T(8,128)S(1)} %copy.36, s32[5120]{0:T(1024)S(1)} %broadcast_clamp_fusion), kind=kCustom, calls=%fused_computation.1 | custom fusion | bytes 10506240 | tf_op jit(solution)/shard_map/jit(_take)/gather | solution.py:73
  557.8 7.4 %select_convert_fusion = bf16[32,160,256]{2,1,0:T(8,128)(2,1)} fusion(f32[32,160,256]{2,1,0:T(8,128)} %all-to-all-done.1, f32[32,160,256]{2,1,0:T(8,128)} %bitcast.106, pred[32,160]{1,0:T(8,128)(4,1)S(1)} %get-tuple-element.51, pred[32,160]{1,0:T(8,128)(4,1)S(1)} %bitcast.117), kind=kLoop, calls=%fused_computation.10 | loop fusion | flops 5242880 | bytes 13117440 | tf_op jit(solution)/shard_map/convert_element_type | solution.py:74
  (57 shorter events, 7.1 us)
Async XLA Ops:
  7.2 281.9 %copy-start = (f32[1024,256]{1,0:T(8,128)S(1)}, f32[1024,256]{1,0:T(8,128)}, u32[]{:S(2)}) copy-start(f32[1024,256]{1,0:T(8,128)} %param.14) | copy-start | bytes 3145732
  7.2 281.8 %all-reduce.3.cloned.1.call-start = ((), (), s32[]{:S(2)}) async-start(), calls=%async_computation.3 | async-start | bytes 8388608 | tf_op jit(solution)/shard_map/psum | solution.py:30
  17.3 0.7 copy-start.2
  17.3 1.0 copy-start.1
  48.8 392.8 %all-to-all-start = ((s32[32,1,160]{2,1,0:T(1,128)}), s32[32,1,160]{2,1,0:T(1,128)S(1)}, u32[]{:S(2)}, u32[]{:S(2)}) async-start(s32[32,1,160]{2,1,0:T(1,128)} %all_to_all.15), calls=%async_computation | async-start | bytes 65536 | tf_op jit(solution)/shard_map/all_to_all | solution.py:69
  441.6 28.9 %all-to-all-start.2 = ((s32[32,1,160]{2,1,0:T(1,128)}), s32[32,1,160]{2,1,0:T(1,128)S(1)}, u32[]{:S(2)}, u32[]{:S(2)}) async-start(s32[32,1,160]{2,1,0:T(1,128)} %all_to_all.18), calls=%async_computation.2 | async-start | bytes 65536 | tf_op jit(solution)/shard_map/all_to_all | solution.py:70
  470.5 87.3 %all-to-all-start.1 = ((f32[32,160,256]{2,1,0:T(8,128)}), f32[32,160,256]{2,1,0:T(8,128)}, u32[]{:S(2)}, u32[]{:S(2)}) async-start(f32[32,160,256]{2,1,0:T(8,128)} %bitcast.107), calls=%async_computation.1 | async-start | bytes 10485760 | tf_op jit(solution)/shard_map/all_to_all | solution.py:68
Sparse Core Ops, SparseCore 0:
  17.4 271.5 all-reduce.2
where the time goes:
time: 580 us; the launch traced here: 572 us
  waiting for transfers between devices  224 us (39%)
  other arithmetic  159 us (27%)
  local copies, waits for them, and re-layouts  76.8 us (13%)
  matrix products  44.1 us (8%)
  between operations  30.1 us (5%)
  starting transfers between devices  22 us (4%)
  blocking collectives  16.2 us (3%)
    psum x1, waiting for transfers between devices, shards(): moment = lax.psum(partial_value, ('group', 'dev'))  224 us
    another operation x13, other arithmetic, orthonormal(): factor = jnp.linalg.cholesky(gram_matrix)  68.5 us
    another operation x5, other arithmetic, orthonormal(): return jax.scipy.linalg.solve_triangular(factor, product.T, lower=True).T  39.8 us
    scatter-add x1, other arithmetic, shards(): jax.ops.segment_sum(filled_flat, jnp.maximum(arrived_ids, 0).reshape(-1),...  33.2 us
    gather x1, local copies, waits for them, and re-layouts, shards(): encoded = values - jnp.take(offsets, clamped, axis=0)  20 us
    psum x1, blocking collectives, shards(): list_counts = lax.psum(tallies, 'group').astype(jnp.int32)  16.2 us
    scatter x1, local copies, waits for them, and re-layouts, shards(): coded_buffer = jnp.zeros((owner_total * capacity, code_width), jnp.float3...  12.1 us
    gather x1, local copies, waits for them, and re-layouts, shards(): slot_ids = jnp.take(list_slot, list_ids)  11.8 us
  transfers between devices with their start and end apart: 4, of which 1 were waited for; matrix products, arithmetic and copies ran while one was open for 45% of the time, Pallas kernels for 0%

commit v1 on v0

v1 whole, which is shorter than its diff:
```python
import functools
import jax, jax.numpy as jnp
from jax import lax
from jax.experimental import pallas as pl
from jax.experimental.pallas import tpu as pltpu
MESH = pl.DeviceIdType.MESH
from jax.sharding import PartitionSpec as P
NX, NY, NZ = 4, 4, 8
HALF, PART, MID, LOW = 2304, 1152, 288, 72


def reduce_kernel(part_ref, out_ref, core_buf, big_buf, mid_buf, tile_buf, core_s, core_r, big_s, big_r, mid_s, mid_r,
                  tile_s, tile_r, up_s, up_r):
    z = lax.axis_index("group")
    dev = lax.axis_index("dev")
    x, y, c = dev // 8, (dev // 2) % 4, dev % 2

    def at(xx, yy, cc, zz):
        return (zz, (xx * 4 + yy) * 2 + cc)

    other = at(x, y, 1 - c, z)
    along_x = [at((x + d) % 4, y, c, z) for d in (1, 2, 3)]
    along_y = [at(x, (y + d) % 4, c, z) for d in (1, 2, 3)]
    along_z = [at(x, y, c, (z + d) % 8) for d in range(1, 8)]
    barrier = pltpu.get_barrier_semaphore()
    for peer in [other] + along_x + along_y + along_z:
        pl.semaphore_signal(barrier, inc=1, device_id=peer, device_id_type=MESH)
    pl.semaphore_wait(barrier, 14)

    def send(src, dst, s, r, peer):
        copy = pltpu.make_async_remote_copy(src_ref=src, dst_ref=dst, send_sem=s, recv_sem=r, device_id=peer,
                                            device_id_type=MESH)
        copy.start()
        return copy

    def rows(ref, start, size):
        return ref.at[pl.ds(pl.multiple_of(start, 8), size)]

    mine, theirs = c * HALF, (1 - c) * HALF
    first = [(x, along_x), (y, along_y)]
    second = [(y, along_y), (x, along_x)]
    core = [send(rows(part_ref, theirs + p * PART, PART), core_buf.at[p], core_s.at[p], core_r.at[p], other)
            for p in range(2)]
    big = [[], []]
    for p in range(2):
        core[p].wait_recv()
        core_buf[p] = core_buf[p] + part_ref[pl.ds(pl.multiple_of(mine + p * PART, 8), PART)]
        pos, peers = first[p]
        for d in (1, 2, 3):
            big[p].append(send(rows(core_buf.at[p], ((pos + d) % 4) * MID, MID), big_buf.at[p, d - 1],
                               big_s.at[p, d - 1], big_r.at[p, d - 1], peers[d - 1]))
    mid = [[], []]
    for p in range(2):
        for copy in big[p]:
            copy.wait_recv()
        pos, peers = first[p]
        own = core_buf[p, pl.ds(pl.multiple_of(pos * MID, 8), MID)]
        big_buf[p, 3] = (own + big_buf[p, 0]) + (big_buf[p, 1] + big_buf[p, 2])
        pos, peers = second[p]
        for d in (1, 2, 3):
            mid[p].append(send(rows(big_buf.at[p, 3], ((pos + d) % 4) * LOW, LOW), mid_buf.at[p, d - 1],
                               mid_s.at[p, d - 1], mid_r.at[p, d - 1], peers[d - 1]))
    tile = [[], []]
    for p in range(2):
        for copy in mid[p]:
            copy.wait_recv()
        pos, peers = second[p]
        own = big_buf[p, 3, pl.ds(pl.multiple_of(pos * LOW, 8), LOW)]
        mid_buf[p, 3] = (own + mid_buf[p, 0]) + (mid_buf[p, 1] + mid_buf[p, 2])
        for d in range(1, 8):
            tile[p].append(send(rows(mid_buf.at[p, 3], ((z + d) % 8) * 8, 8), tile_buf.at[p, d - 1, 0],
                                tile_s.at[p, d - 1, 0], tile_r.at[p, d - 1, 0], along_z[d - 1]))
            tile[p].append(send(mid_buf.at[p, 3, pl.ds(64, 8)], tile_buf.at[p, d - 1, 1],
                                tile_s.at[p, d - 1, 1], tile_r.at[p, d - 1, 1], along_z[d - 1]))
    up = [[], []]

    def spread(p, start, size, peers, base):
        for i, peer in enumerate(peers):
            up[p].append(send(rows(out_ref, start, size), rows(out_ref, start, size), up_s.at[p, base + i],
                              up_r.at[p, base + i], peer))

    start = []
    for p in range(2):
        for copy in tile[p]:
            copy.wait_recv()
        begin = mine + p * PART + first[p][0] * MID + second[p][0] * LOW
        start.append(begin)
        own = mid_buf[p, 3, pl.ds(pl.multiple_of(z * 8, 8), 8)]
        last = mid_buf[p, 3, pl.ds(64, 8)]
        for d in range(7):
            own = own + tile_buf[p, d, 0]
        out_ref[pl.ds(pl.multiple_of(begin + z * 8, 8), 8)] = own
        seq = [last] + [tile_buf[p, d, 1] for d in range(7)]
        tot = jnp.zeros((8, 128), jnp.float32)
        for k in range(8):
            term = seq[0]
            for d in range(1, 8):
                term = jnp.where((z - k + 8) % 8 == d, seq[d], term)
            tot = tot + term
        out_ref[pl.ds(pl.multiple_of(begin + 64, 8), 8)] = tot
        spread(p, begin + z * 8, 8, along_z, 0)
    for p in range(2):
        for copy in up[p][0:7]:
            copy.wait_recv()
        spread(p, start[p], LOW, second[p][1], 7)
    for p in range(2):
        for copy in up[p][7:10]:
            copy.wait_recv()
        spread(p, mine + p * PART + first[p][0] * MID, MID, first[p][1], 10)
    for p in range(2):
        for copy in up[p][10:13]:
            copy.wait_recv()
        spread(p, mine + p * PART, PART, [other], 13)
    for p in range(2):
        up[p][13].wait_recv()
    for p in range(2):
        for copy in [core[p]] + big[p] + mid[p] + tile[p] + up[p]:
            copy.wait_send()


def reduce_moment(part):
    sem = pltpu.SemaphoreType.DMA
    return pl.pallas_call(
        reduce_kernel,
        out_shape=jax.ShapeDtypeStruct(part.shape, jnp.float32),
        in_specs=[pl.BlockSpec(memory_space=pltpu.VMEM)],
        out_specs=pl.BlockSpec(memory_space=pltpu.VMEM),
        scratch_shapes=[
            pltpu.VMEM((2, PART, 128), jnp.float32),
            pltpu.VMEM((2, 4, MID, 128), jnp.float32),
            pltpu.VMEM((2, 4, LOW, 128), jnp.float32),
            pltpu.VMEM((2, 7, 2, 8, 128), jnp.float32),
            sem((2,)), sem((2,)), sem((2, 3)), sem((2, 3)), sem((2, 3)), sem((2, 3)),
            sem((2, 7, 2)), sem((2, 7, 2)), sem((2, 14)), sem((2, 14)),
        ],
        compiler_params=pltpu.CompilerParams(collective_id=0, has_side_effects=True, vmem_limit_bytes=32 * 2**20),
        cost_estimate=pl.CostEstimate(flops=10**6, bytes_accessed=10**8, transcendentals=0),
        name="reduce_moment",
    )(part)


CAP_OF = 160


def dot(a, b, dims=(((1,), (0,)), ((), ()))):
    return lax.dot_general(a, b, dims, preferred_element_type=jnp.float32)


def halves(v):
    top = v.astype(jnp.bfloat16)
    return top, (v - top.astype(jnp.float32)).astype(jnp.bfloat16)


def vmem():
    return pl.BlockSpec(memory_space=pltpu.VMEM)


def smem():
    return pl.BlockSpec(memory_space=pltpu.SMEM)


def limits():
    return pltpu.CompilerParams(vmem_limit_bytes=48 * 2**20)


NT = (((1,), (1,)), ((), ()))
TN = (((0,), (0,)), ((), ()))


def place_kernel(lists_dev, cap, list_ref, source_ref, table_ref, pos_ref, dest_ref):
    count = list_ref.shape[1]
    owners = dest_ref.shape[0]
    table_rows = table_ref.shape[0]
    ids = list_ref[...]
    sub = lax.broadcasted_iota(jnp.int32, (table_rows, count), 0)
    row_hit = (sub == ids // 128).astype(jnp.bfloat16)
    table = table_ref[...]
    high = dot((table // 256).astype(jnp.float32).astype(jnp.bfloat16), row_hit, TN)
    low = dot((table % 256).astype(jnp.float32).astype(jnp.bfloat16), row_hit, TN)
    lane = lax.broadcasted_iota(jnp.int32, (128, count), 0)
    slot = jnp.sum(jnp.where(lane == ids % 128, high * 256.0 + low, 0.0), axis=0, keepdims=True).astype(jnp.int32)
    owner = slot // lists_dev
    local = slot % lists_dev
    owner_hit = lax.broadcasted_iota(jnp.int32, (owners, count), 0) == owner
    owner_one = owner_hit.astype(jnp.float32).astype(jnp.bfloat16)
    width = 256
    before = (
        lax.broadcasted_iota(jnp.int32, (width, width), 0) < lax.broadcasted_iota(jnp.int32, (width, width), 1)
    ).astype(jnp.float32).astype(jnp.bfloat16)
    seen = jnp.zeros((owners, 1), jnp.float32)
    ranks = []
    for k in range(count // width):
        part = owner_one[:, k * width:(k + 1) * width]
        prior = dot(part, before) + seen
        part = part.astype(jnp.float32)
        ranks.append(jnp.sum(prior * part, axis=0, keepdims=True))
        seen = seen + jnp.sum(part, axis=1, keepdims=True)
    rank = jnp.concatenate(ranks, axis=1).astype(jnp.int32)
    pos_ref[...] = owner * cap + rank
    rank_hit = lax.broadcasted_iota(jnp.int32, (cap, count), 0) == rank
    source = source_ref[...]

    def collect(value):
        picked = jnp.where(rank_hit, value.astype(jnp.float32), 0.0).astype(jnp.bfloat16)
        return dot(owner_one, picked, NT)

    filled = collect(jnp.ones((1, count), jnp.int32)) > 0.5
    local_at = collect(local // 256) * 256.0 + collect(local % 256)
    source_at = collect(source // 16384) * 16384.0 + collect((source // 128) % 128) * 128.0 + collect(source % 128)
    dest_ref[:, 0:cap] = jnp.where(filled, local_at, -1.0).astype(jnp.int32)
    dest_ref[:, 256:256 + cap] = jnp.where(filled, source_at, -1.0).astype(jnp.int32)


def place(list_ids, source_ids, list_slot, owners, lists_dev, cap):
    count = list_ids.shape[0]
    return pl.pallas_call(
        functools.partial(place_kernel, lists_dev, cap),
        out_shape=(jax.ShapeDtypeStruct((1, count), jnp.int32), jax.ShapeDtypeStruct((owners, 512), jnp.int32)),
        in_specs=[vmem(), vmem(), vmem()],
        out_specs=(vmem(), vmem()),
        compiler_params=limits(),
        name="place",
    )(list_ids.reshape(1, count), source_ids.reshape(1, count), list_slot.reshape(-1, 128))


def moment_kernel(x_ref, out_ref):
    step = pl.program_id(0)

    @pl.when(step == 0)
    def _():
        out_ref[...] = jnp.zeros_like(out_ref)

    for i in range(4):
        left = x_ref[:, i * 256:(i + 1) * 256].T
        for j in range(i + 1):
            square = dot(left, x_ref[:, j * 256:(j + 1) * 256])
            for a in range(2):
                for b in range(2):
                    row, col = 2 * i + a, 2 * j + b
                    if col <= row:
                        at = (row * (row + 1) // 2 + col) * 128
                        out_ref[at:at + 128, :] += square[a * 128:(a + 1) * 128, b * 128:(b + 1) * 128]


def local_moment(x):
    steps = 4
    return pl.pallas_call(
        moment_kernel,
        out_shape=jax.ShapeDtypeStruct((4608, 128), jnp.float32),
        grid=(steps,),
        in_specs=[pl.BlockSpec((x.shape[0] // steps, x.shape[1]), lambda s: (s, 0))],
        out_specs=pl.BlockSpec((4608, 128), lambda s: (0, 0)),
        compiler_params=limits(),
        name="local_moment",
    )(x)


def project_kernel(tri_ref, start_ref, x_ref, pos_ref, out_ref, basis_ref, gram_ref, m_hi, m_lo, z_ref):
    eye = lax.broadcasted_iota(jnp.int32, (128, 128), 0) == lax.broadcasted_iota(jnp.int32, (128, 128), 1)
    peak = jnp.zeros((128, 128), jnp.float32)
    for i in range(8):
        for j in range(i + 1):
            at = (i * (i + 1) // 2 + j) * 128
            block = tri_ref[at:at + 128, :]
            hi, lo = halves(block)
            m_hi[i * 128:(i + 1) * 128, j * 128:(j + 1) * 128] = hi
            m_lo[i * 128:(i + 1) * 128, j * 128:(j + 1) * 128] = lo
            if i != j:
                hi, lo = halves(block.T)
                m_hi[j * 128:(j + 1) * 128, i * 128:(i + 1) * 128] = hi
                m_lo[j * 128:(j + 1) * 128, i * 128:(i + 1) * 128] = lo
            else:
                peak = jnp.maximum(peak, jnp.where(eye, block, 0.0))
    scale = 1.0 / jnp.max(jnp.max(peak, axis=0, keepdims=True), axis=1, keepdims=True)
    width = start_ref.shape[1]

    def times_moment(v):
        hi, lo = halves(v * scale)
        both = dot(m_hi[...], jnp.concatenate([hi, lo], axis=1))
        return (both[:, :width] + both[:, width:]) + dot(m_lo[...], hi)

    product = times_moment(times_moment(start_ref[...]))
    product = product * lax.rsqrt(jnp.sum(product * product, axis=0, keepdims=True))
    hi, lo = halves(product)
    basis_ref[:, :width] = hi
    basis_ref[:, width:] = lo
    cross = dot(hi, basis_ref[...], TN)
    mixed = cross[:, width:]
    gram_ref[...] = cross[:, :width] + (mixed + mixed.T)
    step = 256

    @pl.loop(0, x_ref.shape[0] // step)
    def _(k):
        at = pl.ds(pl.multiple_of(k * step, step), step)
        both = dot(x_ref[at, :], basis_ref[...])
        z_ref[at, :] = both[:, :width] + both[:, width:]

    @pl.loop(0, x_ref.shape[0] // 16)
    def _(k):
        for u in range(16):
            out_ref[pl.ds(pos_ref[0, k * 16 + u], 1), :] = z_ref[pl.ds(k * 16 + u, 1), :]


def project(tri, start, x, pos, slots):
    feature, width = start.shape
    return pl.pallas_call(
        project_kernel,
        out_shape=(
            jax.ShapeDtypeStruct((slots, width), jnp.float32),
            jax.ShapeDtypeStruct((feature, 2 * width), jnp.bfloat16),
            jax.ShapeDtypeStruct((width, width), jnp.float32),
        ),
        in_specs=[vmem(), vmem(), vmem(), smem()],
        out_specs=(vmem(), vmem(), vmem()),
        scratch_shapes=[
            pltpu.VMEM((feature, feature), jnp.bfloat16),
            pltpu.VMEM((feature, feature), jnp.bfloat16),
            pltpu.VMEM((x.shape[0], width), jnp.float32),
        ],
        compiler_params=limits(),
        cost_estimate=pl.CostEstimate(flops=10**10, bytes_accessed=2 * 10**7, transcendentals=0),
        name="project",
    )(tri, start, x, pos)


def factor_kernel(gram_ref, inverse_ref, pivot_ref, aug):
    size = gram_ref.shape[0]
    block = 32
    panel = 8
    aug[:, :size] = gram_ref[...]
    aug[:, size:] = (
        lax.broadcasted_iota(jnp.int32, (size, size), 0) == lax.broadcasted_iota(jnp.int32, (size, size), 1)
    ).astype(jnp.float32)
    row_at = lax.broadcasted_iota(jnp.int32, (block, 128), 0)
    lane_at = lax.broadcasted_iota(jnp.int32, (block, 128), 1)
    least = jnp.full((1, 128), 1e30, jnp.float32)
    for b in range(size // block):
        lo, hi = b * block, (b + 1) * block
        square = aug[lo:hi, lo:hi]
        unit = (row_at[:, :block] == lane_at[:, :block]).astype(jnp.float32)
        work = jnp.concatenate([square, unit, jnp.zeros((block, 128 - 2 * block), jnp.float32)], axis=1)
        for p in range(block // panel):
            cols = [
                jnp.broadcast_to(work[:, p * panel + j:p * panel + j + 1], (block, 128)) for j in range(panel)
            ]
            for j in range(panel):
                k = p * panel + j
                pivot = cols[j][k:k + 1, :]
                least = jnp.minimum(least, pivot)
                root = lax.rsqrt(pivot)
                column = jnp.where(row_at > k, cols[j] * root, 0.0)
                for jj in range(j + 1, panel):
                    kk = p * panel + jj
                    cols[jj] = cols[jj] - column * column[kk:kk + 1, :]
                row = work[k:k + 1, :] * root
                work = jnp.where(row_at == k, row, work - column * row)
        inverse = work[:, block:2 * block]
        rows = lax.dot_general(inverse, aug[lo:hi, :], (((1,), (0,)), ((), ())), precision=lax.Precision.HIGHEST,
                               preferred_element_type=jnp.float32)
        aug[lo:hi, :] = rows
        if hi < size:
            below = rows[:, hi:size].T
            aug[hi:, :] -= lax.dot_general(below, rows, (((1,), (0,)), ((), ())), precision=lax.Precision.HIGHEST,
                                           preferred_element_type=jnp.float32)
    whole = aug[:, size:].T
    top, bottom = halves(whole)
    inverse_ref[:, :size] = top
    inverse_ref[:, size:] = bottom
    pivot_ref[...] = least


def factor(gram):
    size = gram.shape[0]
    return pl.pallas_call(
        factor_kernel,
        out_shape=(
            jax.ShapeDtypeStruct((size, 2 * size), jnp.bfloat16),
            jax.ShapeDtypeStruct((1, 128), jnp.float32),
        ),
        in_specs=[vmem()],
        out_specs=(vmem(), vmem()),
        scratch_shapes=[pltpu.VMEM((size, 2 * size), jnp.float32)],
        compiler_params=limits(),
        cost_estimate=pl.CostEstimate(flops=10**9, bytes_accessed=10**7, transcendentals=0),
        name="factor",
    )(gram)


def offset_kernel(c_ref, basis_ref, id_ref, out_ref, z_ref):
    width = out_ref.shape[1]
    step = 256

    @pl.loop(0, c_ref.shape[0] // step)
    def _(k):
        at = pl.ds(pl.multiple_of(k * step, step), step)
        both = dot(c_ref[at, :], basis_ref[...])
        z_ref[at, :] = both[:, :width] + both[:, width:]

    @pl.loop(0, out_ref.shape[0] // 16)
    def _(k):
        for u in range(16):
            at = jnp.maximum(id_ref[k * 16 + u], 0)
            out_ref[pl.ds(k * 16 + u, 1), :] = z_ref[pl.ds(at, 1), :]


def offsets_at(centroids, basis, ids):
    width = basis.shape[1] // 2
    return pl.pallas_call(
        offset_kernel,
        out_shape=jax.ShapeDtypeStruct((ids.shape[0], width), jnp.float32),
        in_specs=[vmem(), vmem(), smem()],
        out_specs=vmem(),
        scratch_shapes=[pltpu.VMEM((centroids.shape[0], width), jnp.float32)],
        compiler_params=limits(),
        cost_estimate=pl.CostEstimate(flops=10**10, bytes_accessed=10**7, transcendentals=0),
        name="offsets",
    )(centroids, basis, ids)


def finish_kernel(z_ref, off_ref, id_ref, inverse_ref, out_ref):
    width = z_ref.shape[1]
    hi, lo = halves(z_ref[...] - off_ref[...])
    both = dot(hi, inverse_ref[...])
    code = (both[:, :width] + both[:, width:]) + dot(lo, inverse_ref[:, :width])
    out_ref[...] = jnp.where(id_ref[...] >= 0, code, 0.0).astype(jnp.bfloat16)


def finish(z, off, ids, inverse):
    slots, width = z.shape
    step = 512
    return pl.pallas_call(
        finish_kernel,
        out_shape=jax.ShapeDtypeStruct((slots, width), jnp.bfloat16),
        grid=(slots // step,),
        in_specs=[
            pl.BlockSpec((step, width), lambda s: (s, 0)),
            pl.BlockSpec((step, width), lambda s: (s, 0)),
            pl.BlockSpec((step, 1), lambda s: (s, 0)),
            pl.BlockSpec((width, 2 * width), lambda s: (0, 0)),
        ],
        out_specs=pl.BlockSpec((step, width), lambda s: (s, 0)),
        compiler_params=limits(),
        cost_estimate=pl.CostEstimate(flops=2 * 10**9, bytes_accessed=13 * 10**6, transcendentals=0),
        name="finish",
    )(z, off, ids.reshape(slots, 1), inverse)


def tally_kernel(id_ref, out_ref):
    ids = id_ref[...]
    count = ids.shape[1]
    high = lax.broadcasted_iota(jnp.int32, (16, count), 0) == jnp.where(ids >= 0, ids // 128, -1)
    low = lax.broadcasted_iota(jnp.int32, (128, count), 0) == ids % 128
    out_ref[...] = dot(high.astype(jnp.float32).astype(jnp.bfloat16), low.astype(jnp.float32).astype(jnp.bfloat16), NT)


def tally(ids):
    return pl.pallas_call(
        tally_kernel,
        out_shape=jax.ShapeDtypeStruct((16, 128), jnp.float32),
        in_specs=[vmem()],
        out_specs=vmem(),
        compiler_params=limits(),
        cost_estimate=pl.CostEstimate(flops=10**7, bytes_accessed=10**6, transcendentals=0),
        name="tally",
    )(ids.reshape(1, -1))


exact_mode = lax.Precision.HIGHEST
PIVOT_LEAST = 1.0 / 64.0


def orthonormal(product):
    gram_matrix = jnp.dot(product.T, product, precision=exact_mode, preferred_element_type=jnp.float32)
    lower = jnp.linalg.cholesky(gram_matrix)
    return jax.scipy.linalg.solve_triangular(lower, product.T, lower=True).T


def careful(tri, start, x, centroids, pos, ids):
    owners = lax.axis_size("dev")
    slots = ids.shape[0]
    grid = [[None] * 8 for _ in range(8)]
    for i in range(8):
        for j in range(i + 1):
            at = (i * (i + 1) // 2 + j) * 128
            grid[i][j] = tri[at:at + 128]
            grid[j][i] = tri[at:at + 128].T
    moment = jnp.block(grid)
    basis = start
    for sweep in range(2):
        product = jnp.dot(moment, basis, precision=exact_mode, preferred_element_type=jnp.float32)
        basis = orthonormal(product)
    width = start.shape[1]
    projected = jnp.dot(x, basis, precision=exact_mode, preferred_element_type=jnp.float32)
    sent = jnp.zeros((slots, width), jnp.float32).at[pos.reshape(-1)].set(projected)
    sent = sent.reshape(owners, slots // owners, width)
    values = lax.all_to_all(sent, "dev", split_axis=0, concat_axis=0, tiled=True).reshape(slots, width)
    offsets = jnp.dot(centroids, basis, precision=exact_mode, preferred_element_type=jnp.float32)
    code = values - jnp.take(offsets, jnp.maximum(ids, 0), axis=0)
    return jnp.where(ids[:, None] >= 0, code, 0.0).astype(jnp.bfloat16)


def shards(corpus_rows, list_ids, source_ids, list_slot, centroids, start_basis):
    owners = lax.axis_size("dev")
    lists_dev = centroids.shape[0]
    cap = CAP_OF
    slots = owners * cap
    pos, dest = place(list_ids, source_ids, list_slot, owners, lists_dev, cap)
    arrived = lax.all_to_all(dest, "dev", split_axis=0, concat_axis=0, tiled=True)
    tri = reduce_moment(local_moment(corpus_rows))
    sent, basis, gram = project(tri, start_basis, corpus_rows, pos, slots)
    width = start_basis.shape[1]
    values = lax.all_to_all(
        sent.reshape(owners, cap, width), "dev", split_axis=0, concat_axis=0, tiled=True
    ).reshape(slots, width)
    ids = arrived[:, :cap].reshape(slots)
    row_sources = arrived[:, 256:256 + cap].reshape(slots)
    tallies = lax.all_gather(tally(ids), "group")
    inverse, pivots = factor(gram)
    off = offsets_at(centroids, basis, ids)
    row_codes = lax.cond(
        jnp.min(pivots) >= PIVOT_LEAST,
        lambda: finish(values, off, ids, inverse),
        lambda: careful(tri, start_basis, corpus_rows, centroids, pos, ids),
    )
    list_counts = jnp.sum(tallies, axis=0).astype(jnp.int32).reshape(lists_dev)
    return row_codes, row_sources, list_counts


def solution(mesh):
    placed = (
        P(("group", "dev"), None),
        P(("group", "dev")),
        P(("group", "dev")),
        P(),
        P("dev", None),
        P(),
    )
    return jax.shard_map(
        shards,
        mesh=mesh,
        in_specs=placed,
        out_specs=(P(("group", "dev"), None), P(("group", "dev")), P("dev")),
        check_vma=False,
    )
```

time: 580 us -> 183 us (0.32); the launches traced: 572 us -> 182 us
  waiting for transfers between devices: 224 us -> 3.49 us
  other arithmetic: 159 us -> 1.21 us
  Pallas kernels: 0 us -> 128 us
  local copies, waits for them, and re-layouts: 76.8 us -> 7.81 us
  matrix products: 44.1 us -> 0 us
  between operations: 30.1 us -> 1.4 us
  blocking collectives: 16.2 us -> 24.6 us
  starting transfers between devices: 22 us -> 15.5 us
    psum x1 -> x0, waiting for transfers between devices: 224 us -> none  [shards(): moment = lax.psum(partial_value, ('group', 'dev'))]
    pallas_call x0 -> x8, Pallas kernels: none -> 128 us  [the longest x1 47.9 us: reduce_moment(): pl.pallas_call(reduce_kernel, out_shape=jax.ShapeDtypeStruct(part.shape,...]
    another operation x20 -> x0, other arithmetic: 118 us -> none  [the longest x13 68.5 us: orthonormal(): factor = jnp.linalg.cholesky(gram_matrix)]
    dot_general x7 -> x0, matrix products: 38.6 us -> none  [the longest x2 10.9 us: shards(): jnp.dot(moment, basis_now, precision=exact_mode, preferred_element_type=j...]
    scatter-add x1 -> x0, other arithmetic: 33.2 us -> none  [shards(): jax.ops.segment_sum(filled_flat, jnp.maximum(arrived_ids, 0).reshape(-1),...]
    gather x2 -> x0, local copies, waits for them, and re-layouts: 31.8 us -> none  [the longest x1 20 us: shards(): encoded = values - jnp.take(offsets, clamped, axis=0)]
    scatter x3 -> x0, local copies, waits for them, and re-layouts: 28.4 us -> none  [the longest x1 12.1 us: shards(): coded_buffer = jnp.zeros((owner_total * capacity, code_width), jnp.float3...]
    all_gather x0 -> x1, blocking collectives: none -> 24.6 us  [shards(): tallies = lax.all_gather(tally(ids), 'group')]
  transfers between devices with their start and end apart: 4 -> 2, of which waited for: 1 -> 1; matrix products, arithmetic and copies ran while one was open for 45% -> 1% of each run, Pallas kernels for 0% -> 63%
where the time goes in v1:
time: 183 us; the launch traced here: 182 us
  Pallas kernels  128 us (70%)
  blocking collectives  24.6 us (13%)
  starting transfers between devices  15.5 us (8%)
  local copies, waits for them, and re-layouts  7.81 us (4%)
  waiting for transfers between devices  3.49 us (2%)
    pallas_call x1, Pallas kernels, reduce_moment(): pl.pallas_call(reduce_kernel, out_shape=jax.ShapeDtypeStruct(part.shape,...  47.9 us
    pallas_call x1, Pallas kernels, offsets_at(): pl.pallas_call(offset_kernel, out_shape=jax.ShapeDtypeStruct((ids.shape[0...  28 us
    all_gather x1, blocking collectives, shards(): tallies = lax.all_gather(tally(ids), 'group')  24.6 us
    pallas_call x1, Pallas kernels, project(): pl.pallas_call(project_kernel, out_shape=(jax.ShapeDtypeStruct((slots, wi...  21.1 us
    pallas_call x1, Pallas kernels, factor(): pl.pallas_call(factor_kernel, out_shape=(jax.ShapeDtypeStruct((size, 2 *...  12 us
    pallas_call x1, Pallas kernels, finish(): pl.pallas_call(finish_kernel, out_shape=jax.ShapeDtypeStruct((slots, widt...  10.1 us
    all_to_all x1, starting transfers between devices, shards(): lax.all_to_all(sent.reshape(owners, cap, width), 'dev', split_axis=0, con...  7.97 us
    all_to_all x1, starting transfers between devices, shards(): lax.all_to_all(dest, 'dev', split_axis=0, concat_axis=0, tiled=True)  7.52 us
  transfers between devices with their start and end apart: 2, of which 1 were waited for; matrix products, arithmetic and copies ran while one was open for 1% of the time, Pallas kernels for 63%

profile of v1, /device:TPU:8, one launch (start us, length us, event | category | flops | bytes accessed | tf_op | source)
XLA Modules:
  0.0 182.0 jit_solution(5114088635924595091)
XLA Ops:
  0.6 0.0 copy-start
  0.6 0.9 copy-done
  1.6 0.0 copy-start.1
  1.6 0.7 copy-done.1
  2.3 0.0 copy-start.2
  2.3 0.7 copy-done.2
  3.0 2.9 %place.1 = (s32[1,2048]{1,0:T(1,128)S(1)}, s32[32,512]{1,0:T(8,128)S(1)}) custom-call(s32[1,2048]{1,0:T(1,128)S(1)} %bitcast.179, s32[1,2048]{1,0:T(1,128)S(1)} %bitcast.180, s32[512,128]{1,0:T(8,128)S(1)} %bitcast.177), custom_call_target="tpu_custom_call" | custom-call | tf_op jit(solution)/shard_map/place/pallas_call | solution.py:216
  5.9 0.7 copy.118
  6.6 7.5 %all-to-all-start.1 = ((s32[32,1,512]{2,1,0:T(1,128)}), s32[32,1,512]{2,1,0:T(1,128)S(1)}, u32[]{:S(2)}, u32[]{:S(2)}) async-start(s32[32,1,512]{2,1,0:T(1,128)} %copy.118), calls=%async_computation.1 | async-start | bytes 131072 | tf_op jit(solution)/shard_map/all_to_all | solution.py:508
  14.1 0.0 copy-start.5
  14.2 0.0 copy-start.6
  14.2 5.6 %local_moment.1.part_ref = f32[4608,128]{1,0:T(8,128)S(1)} custom-call(bf16[2048,1024]{1,0:T(8,128)(2,1)} %x_ref.3), custom_call_target="tpu_custom_call" | custom-call | tf_op jit(solution)/shard_map/local_moment/pallas_call | solution.py:247
  19.8 47.9 %reduce_moment.1.tri_ref = f32[4608,128]{1,0:T(8,128)S(1)} custom-call(f32[4608,128]{1,0:T(8,128)S(1)} %local_moment.1.part_ref), custom_call_target="tpu_custom_call" | custom-call | flops 1000000 | bytes 100000000 | tf_op jit(solution)/shard_map/reduce_moment/pallas_call | solution.py:123
  67.6 0.0 copy-start.3
  67.6 1.4 copy-done.3
  69.0 0.0 copy-done.5
  69.0 0.0 copy-done.6
  69.0 21.1 %project.1 = (f32[5120,256]{1,0:T(8,128)}, bf16[1024,512]{1,0:T(8,128)(2,1)S(1)}, f32[256,256]{1,0:T(8,128)S(1)}) custom-call(f32[4608,128]{1,0:T(8,128)S(1)} %reduce_moment.1.tri_ref, f32[1024,256]{1,0:T(8,128)S(1)} %copy-done.6, bf16[2048,1024]{1,0:T(8,128)(2,1)S(1)} %copy-done.5, s32[1,2048]{1,0:T(1,128)S(1)} %get-tuple-element.49.pos_ref), custom_call_target="tpu_custom_call" | custom-call | flops 10000000000 | bytes 20000000 | tf_op jit(solution)/shard_map/project/pallas_call | solution.py:306
  90.1 0.0 all-to-all-done.1
  90.1 8.0 %all-to-all-start.2 = ((f32[32,160,256]{2,1,0:T(8,128)}), f32[32,160,256]{2,1,0:T(8,128)}, u32[]{:S(2)}, u32[]{:S(2)}) async-start(f32[32,160,256]{2,1,0:T(8,128)} %bitcast.186), calls=%async_computation.2 | async-start | bytes 10485760 | tf_op jit(solution)/shard_map/all_to_all | solution.py:512
  98.1 12.0 %factor.1 = (bf16[256,512]{1,0:T(8,128)(2,1)}, f32[1,128]{1,0:T(1,128)S(1)}) custom-call(f32[256,256]{1,0:T(8,128)S(1)} %get-tuple-element.50.gram_ref), custom_call_target="tpu_custom_call" | custom-call | flops 1000000000 | bytes 10000000 | tf_op jit(solution)/shard_map/factor/pallas_call | solution.py:374
  110.1 0.6 reduce_min.9
  111.4 0.1 reshape.102.id_ref
  111.5 0.1 reshape_reshape.6.id_ref
  111.6 0.7 reshape.104
  112.3 0.4 tally.1
  112.7 24.6 %all-gather = f32[128,128]{1,0:T(8,128)S(1)} all-gather(f32[16,128]{1,0:T(8,128)S(1)} %tally.1), channel_id=2, replica_groups=mesh['group'=8,'dev'=32] {'group'}, dimensions={0}, use_global_device_ids=true | all-gather | bytes 73728 | tf_op jit(solution)/shard_map/all_gather | solution.py:517
  137.3 0.6 convert_bitcast_fusion
  137.9 0.0 copy-start.4
  137.9 28.0 %offsets.1 = f32[5120,256]{1,0:T(8,128)} custom-call(bf16[2048,1024]{1,0:T(8,128)(2,1)} %c_ref.1, bf16[1024,512]{1,0:T(8,128)(2,1)S(1)} %get-tuple-element.54.basis_ref, s32[5120]{0:T(1024)S(1)} %reshape.102.id_ref), custom_call_target="tpu_custom_call" | custom-call | flops 10000000000 | bytes 10000000 | tf_op jit(solution)/shard_map/offsets/pallas_call | solution.py:408
  166.0 3.5 %all-to-all-done.2 = f32[32,160,256]{2,1,0:T(8,128)} async-done(((f32[32,160,256]{2,1,0:T(8,128)}), f32[32,160,256]{2,1,0:T(8,128)}, u32[]{:S(2)}, u32[]{:S(2)}) %all-to-all-start.2) | async-done | bytes 5242912 | tf_op jit(solution)/shard_map/all_to_all | solution.py:512
  169.4 0.0 copy-done.4
  169.4 12.6 %conditional.1 = (bf16[5120,256]{1,0:T(8,128)(2,1)}) conditional(s32[]{:T(128)} %convert_element_type.13, (s32[32,160]{1,0:T(8,128)S(1)}, s32[1,2048]{1,0:T(1,128)S(1)}, f32[4608,128]{1,0:T(8,128)S(1)}, f32[1024,256]{1,0:T(8,128)}, bf16[2048,1024]{1,0:T(8,128)(2,1)}, /*index=5*/s32[5120]{0:T(1024)S(1)}, bf16[2048,1024]{1,0:T(8,128)(2,1)}) %tuple.87, ...), branch_computations={%region_1.9_spmd, %region_7.10_spmd} | conditional | flops 22253993984 | bytes 124673016 | solution.py:520
  169.4 2.5 %reshape_reshape.7.id_ref = s32[5120,1]{1,0:T(8,128)S(1)} reshape(s32[32,160]{1,0:T(8,128)S(1)} %get-tuple-element.37) | data formatting | bytes 40960 | tf_op jit(solution)/shard_map/cond/branch_1_fun/reshape;reshape | solution.py:445
  171.9 10.1 %finish.1 = bf16[5120,256]{1,0:T(8,128)(2,1)} custom-call(f32[5120,256]{1,0:T(8,128)} %bitcast.54.z_ref, f32[5120,256]{1,0:T(8,128)} %get-tuple-element.36.off_ref, s32[5120,1]{1,0:T(8,128)S(1)} %reshape_reshape.7.id_ref, bf16[256,512]{1,0:T(8,128)(2,1)} %get-tuple-element.38.inverse_ref), custom_call_target="tpu_custom_call" | custom-call | flops 2000000000 | bytes 13000000 | tf_op jit(solution)/shard_map/cond/branch_1_fun/finish/pallas_call | solution.py:431
  (3 shorter events, 0.0 us)
Async XLA Ops:
  0.6 1.0 copy-start
  1.6 0.7 copy-start.1
  2.3 0.7 copy-start.2
  6.6 83.5 %all-to-all-start.1 = ((s32[32,1,512]{2,1,0:T(1,128)}), s32[32,1,512]{2,1,0:T(1,128)S(1)}, u32[]{:S(2)}, u32[]{:S(2)}) async-start(s32[32,1,512]{2,1,0:T(1,128)} %copy.118), calls=%async_computation.1 | async-start | bytes 131072 | tf_op jit(solution)/shard_map/all_to_all | solution.py:508
  14.1 54.9 %copy-start.5 = (bf16[2048,1024]{1,0:T(8,128)(2,1)S(1)}, bf16[2048,1024]{1,0:T(8,128)(2,1)}, u32[]{:S(2)}) copy-start(bf16[2048,1024]{1,0:T(8,128)(2,1)} %x_ref.3) | copy-start | bytes 12582916
  14.2 54.9 %copy-start.6 = (f32[1024,256]{1,0:T(8,128)S(1)}, f32[1024,256]{1,0:T(8,128)}, u32[]{:S(2)}) copy-start(f32[1024,256]{1,0:T(8,128)} %start_ref.1) | copy-start | bytes 3145732
  67.6 1.4 copy-start.3
  90.1 79.3 %all-to-all-start.2 = ((f32[32,160,256]{2,1,0:T(8,128)}), f32[32,160,256]{2,1,0:T(8,128)}, u32[]{:S(2)}, u32[]{:S(2)}) async-start(f32[32,160,256]{2,1,0:T(8,128)} %bitcast.186), calls=%async_computation.2 | async-start | bytes 10485760 | tf_op jit(solution)/shard_map/all_to_all | solution.py:512
  137.9 31.5 %copy-start.4 = (f32[4608,128]{1,0:T(8,128)S(1)}, f32[4608,128]{1,0:T(8,128)}, u32[]{:S(2)}) copy-start(f32[4608,128]{1,0:T(8,128)} %copy-done.3) | copy-start | bytes 7077892
